TPU v7x, 32 devices: a whole 2x2x4 slice. The times are simulated.
32 devices in a mesh: groups: 2 (over y), chol: 4 (over z), walk: 2 (over x), kpt: 2 (over core).
Axes of the slice: x: 2, y: 2, z: 4, core: 2. Of those that a mesh axis runs over, the one named last changes fastest.
Arguments:
- green_blocks: bfloat16 [16, 4, 64, 1024], P(('groups', 'chol', 'walk'), None, 'kpt'), parts along dimension 0, may hold values from -6 to 6
- chol_vectors: bfloat16 [4, 64, 1024, 256], P('chol', 'kpt', 'walk'), may hold values from -0.0234375 to 0.0234375
- aux_fields: float32 [16, 4, 256], P('groups', 'chol'), parts along dimension 0, may hold values from -6 to 6
- orbitals: bfloat16 [16, 64, 768], P(('groups', 'chol', 'walk'), 'kpt'), parts along dimension 0, may hold values from -6 to 6
- transfer_table: int32 [64, 4], replicated, may hold values from 0 to 63, as said below
Outputs:
- force_bias: float32 [16, 4, 256], P('groups', 'chol'), parts along dimension 0
- new_orbitals: bfloat16 [16, 64, 768], P(('groups', 'chol', 'walk'), 'kpt'), parts along dimension 0
There are 2 independent parts, one for each index of `groups`. A program takes and returns all parts, laid end to end along the dimension named above; an argument that names none is the same for every part. Nothing has to cross between parts.
Inputs may be any that keep to these rules, and one draw needn't show every extreme that they name: `transfer_table`: column j holds, for every k-point k = 4**2 kx + 4 ky + kz of the 4 x 4 x 4 grid, the index of k - q_j taken modulo the grid in each component, for 4 distinct transfers q_j; each column is a permutation of the k-points.
All inputs are finite; a program needn't handle non-finite values.
Results may differ from a plain program's by a relative error of at most 0.022.
Values may be sent and summed in bfloat16 or wider, within the bound.
A program may use at most 64 MiB of HBM per device.

v0:
```python
import jax
import jax.numpy as jnp
from jax import lax
from jax.sharding import PartitionSpec as P

NORB = 32
SPOCC = 24
TAYLOR = 4


bias_scale = 0.5


def swap_major(values, first, second):
    leading = values.shape[0] // (first * second)
    grouped = values.reshape((first, second, leading) + values.shape[1:])
    return jnp.swapaxes(grouped, 0, 1).reshape(values.shape)


def per_device(green_blocks, chol_vectors, aux_fields, orbitals, transfer_table):
    chol_count = lax.axis_size("chol")
    walk_count = lax.axis_size("walk")
    walker_dev, transfers, kpt_dev, pair_count = green_blocks.shape
    local_transfers = chol_vectors.shape[0]
    pair_dev = chol_vectors.shape[2]
    channels = chol_vectors.shape[3]
    everyone = aux_fields.shape[0]
    vector_rows = chol_vectors.reshape(local_transfers, kpt_dev * pair_dev, channels)
    arrived = lax.all_to_all(
        lax.all_to_all(green_blocks, "chol", split_axis=1, concat_axis=0, tiled=True),
        "walk",
        split_axis=3,
        concat_axis=0,
        tiled=True,
    )
    mixed_fields = swap_major(aux_fields, chol_count, walk_count)
    partial_bias = jnp.einsum(
        "wqx,qxn->wqn",
        arrived.reshape(everyone, local_transfers, kpt_dev * pair_dev),
        vector_rows,
        preferred_element_type=jnp.float32,
    )
    summed_bias = lax.psum(partial_bias.astype(jnp.bfloat16), ("walk", "kpt")).astype(jnp.float32)
    shifted = (mixed_fields - jnp.clip(-bias_scale * summed_bias, -1.0, 1.0)).astype(jnp.bfloat16)
    operator_rows = jnp.einsum(
        "wqn,qxn->wqx", shifted, vector_rows, preferred_element_type=jnp.float32
    ).astype(jnp.bfloat16)
    mixed_bias, operator_rows = (summed_bias, operator_rows)
    force_bias = swap_major(mixed_bias, walk_count, chol_count)
    outgoing = operator_rows.reshape(everyone, local_transfers, kpt_dev, pair_dev)
    partway = lax.all_to_all(outgoing, "walk", split_axis=0, concat_axis=3, tiled=True)
    returned = lax.all_to_all(partway, "chol", split_axis=0, concat_axis=1, tiled=True)
    kpt_start = lax.axis_index("kpt") * kpt_dev
    local_table = lax.dynamic_slice_in_dim(transfer_table, kpt_start, kpt_dev, 0)
    operator_blocks = returned.reshape(walker_dev, transfers, kpt_dev, NORB, NORB)
    series_term = orbitals
    summed = orbitals.astype(jnp.float32)
    for degree in range(1, TAYLOR + 1):
        gathered = lax.all_gather(series_term, "kpt", axis=1, tiled=True)
        source = jnp.take(gathered, local_table, axis=1).reshape(
            walker_dev, kpt_dev, transfers, NORB, SPOCC
        )
        product = jnp.einsum(
            "wqkij,wkqjc->wkic", operator_blocks, source, preferred_element_type=jnp.float32
        )
        update = (product / degree).reshape(walker_dev, kpt_dev, NORB * SPOCC)
        summed = summed + update
        series_term = update.astype(jnp.bfloat16)
    return (force_bias, summed.astype(jnp.bfloat16))


def solution(mesh):
    placed = (
        P(("groups", "chol", "walk"), None, "kpt", None),
        P("chol", "kpt", "walk", None),
        P("groups", "chol", None),
        P(("groups", "chol", "walk"), "kpt", None),
        P(),
    )
    return jax.shard_map(
        per_device,
        mesh=mesh,
        in_specs=placed,
        out_specs=(P("groups", "chol", None), P(("groups", "chol", "walk"), "kpt", None)),
        check_vma=False,
    )
```

profile of v0, /device:TPU:1, one launch (start us, length us, event | category | flops | bytes accessed | tf_op | source)
XLA Modules:
  0.0 85.4 jit_solution(1025025569208849093)
XLA Ops:
  0.6 12.3 %all_to_all.54 = bf16[1,4,32,1024]{3,2,0,1:T(8,128)(2,1)S(1)} all-to-all(bf16[1,4,32,1024]{3,2,0,1:T(8,128)(2,1)} %bitcast.99), channel_id=1, replica_groups=mesh['groups'=2,'chol'=4,'walk'=2,'kpt'=2] {'chol'}, dimensions={1} | all-to-all | bytes 524288 | tf_op jit(solution)/shard_map/all_to_all | solution.py:30
  13.6 1.7 %reshape.244 = bf16[2,2,32768]{2,1,0:T(2,128)(2,1)} reshape(bf16[1024,1,4,32]{3,2,1,0:T(4,128)(2,1)S(1)} %bitcast.92) | data formatting | bytes 524288
  15.4 3.4 %all-to-all-start.1 = ((bf16[2,2,32768]{2,1,0:T(2,128)(2,1)}), bf16[2,2,32768]{2,1,0:T(2,128)(2,1)S(1)}, u32[]{:S(2)}, u32[]{:S(2)}) async-start(bf16[2,2,32768]{2,1,0:T(2,128)(2,1)} %reshape.244), calls=%async_computation.1 | async-start | bytes 524288 | tf_op jit(solution)/shard_map/all_to_all | solution.py:29
  19.6 3.3 %all-to-all-done.1 = bf16[2,2,32768]{2,1,0:T(2,128)(2,1)S(1)} async-done(((bf16[2,2,32768]{2,1,0:T(2,128)(2,1)}), bf16[2,2,32768]{2,1,0:T(2,128)(2,1)S(1)}, u32[]{:S(2)}, u32[]{:S(2)}) %all-to-all-start.1) | async-done | bytes 262176 | tf_op jit(solution)/shard_map/all_to_all | solution.py:29
  24.2 4.6 %fusion.3 = bf16[8,1,256]{2,0,1:T(8,128)(2,1)S(1)} fusion(bf16[16384,256]{1,0:T(8,128)(2,1)} %bitcast.86, bf16[8,16384]{1,0:T(8,128)(2,1)S(1)} %bitcast.95), kind=kOutput, calls=%fused_computation.13 | convolution fusion | flops 67110912 | bytes 8654848 | tf_op jit(solution)/shard_map/wqx,qxn->wqn/dot_general | solution.py:37
  28.8 9.1 %psum.7 = bf16[8,1,256]{2,0,1:T(8,128)(2,1)S(1)} all-reduce(bf16[8,1,256]{2,0,1:T(8,128)(2,1)S(1)} %fusion.3), channel_id=1, replica_groups=mesh['groups'=2,'chol'=4,'walk'=2,'kpt'=2] {'walk','kpt'}, use_global_device_ids=true, to_apply=%region_0.0 | all-reduce | flops 2048 | bytes 8192 | tf_op jit(solution)/shard_map/psum | solution.py:43
  37.9 5.6 %convolution_convert_fusion = bf16[8,16384]{1,0:T(8,128)(2,1)S(1)} fusion(bf16[16384,256]{1,0:T(8,128)(2,1)} %bitcast.87, f32[8,1,256]{2,0,1:T(8,128)S(1)} %reshape.156, bf16[8,1,256]{2,0,1:T(8,128)(2,1)S(1)} %psum.7), kind=kOutput, calls=%fused_computation.4 | convolution fusion | flops 67250176 | bytes 8663040 | tf_op jit(solution)/shard_map/wqn,qxn->wqx/dot_general | solution.py:45
  43.5 0.8 copy.41
  44.3 3.4 %all-to-all-start.2 = ((bf16[8,1,32,512]{3,2,1,0:T(8,128)(2,1)}), bf16[8,1,32,512]{3,2,1,0:T(8,128)(2,1)S(1)}, u32[]{:S(2)}, u32[]{:S(2)}) async-start(bf16[8,1,32,512]{3,2,1,0:T(8,128)(2,1)} %copy.41), calls=%async_computation.2 | async-start | bytes 524288 | tf_op jit(solution)/shard_map/all_to_all | solution.py:51
  47.8 4.5 %all-to-all-done.2 = bf16[8,1,32,512]{3,2,1,0:T(8,128)(2,1)S(1)} async-done(((bf16[8,1,32,512]{3,2,1,0:T(8,128)(2,1)}), bf16[8,1,32,512]{3,2,1,0:T(8,128)(2,1)S(1)}, u32[]{:S(2)}, u32[]{:S(2)}) %all-to-all-start.2) | async-done | bytes 262176 | tf_op jit(solution)/shard_map/all_to_all | solution.py:51
  52.5 0.9 %all_to_all.48 = bf16[4,1,32,1024]{3,2,1,0:T(8,128)(2,1)} reshape(bf16[4,1,32,2,512]{4,3,2,0,1:T(2,128)(2,1)S(1)} %copy.42) | data formatting | bytes 524288 | tf_op jit(solution)/shard_map/all_to_all | solution.py:51
  53.4 3.4 %all-to-all-start.3 = ((bf16[4,1,32,1024]{3,2,1,0:T(8,128)(2,1)}), bf16[4,1,32,1024]{3,2,1,0:T(8,128)(2,1)S(1)}, u32[]{:S(2)}, u32[]{:S(2)}) async-start(bf16[4,1,32,1024]{3,2,1,0:T(8,128)(2,1)} %all_to_all.48), calls=%async_computation.3 | async-start | bytes 524288 | tf_op jit(solution)/shard_map/all_to_all | solution.py:52
  57.1 3.2 %all_gather.12 = bf16[1,64,768]{2,1,0:T(8,128)(2,1)S(1)} all-gather(bf16[1,32,768]{2,1,0:T(8,128)(2,1)S(1)} %copy-done), channel_id=1, replica_groups=mesh['groups'=2,'chol'=4,'walk'=2,'kpt'=2] {'kpt'}, dimensions={1}, use_global_device_ids=true | all-gather | bytes 147456 | tf_op jit(solution)/shard_map/all_gather | solution.py:59
  60.3 0.9 %gather_fusion = bf16[128,768]{1,0:T(8,128)(2,1)S(1)} fusion(bf16[64,768]{1,0:T(8,128)(2,1)S(1)} %bitcast.88, s32[1024]{0:T(1024)S(1)} %pad_clamp_fusion), kind=kCustom, calls=%fused_computation.clone | custom fusion | bytes 393728 | tf_op jit(solution)/shard_map/jit(_take)/gather | solution.py:60
  61.3 1.7 %reshape.160 = bf16[32,4,32,24]{3,2,0,1:T(8,128)(2,1)S(1)} reshape(bf16[1,32,4,768]{3,1,2,0:T(8,128)(2,1)S(1)} %copy_select_fusion.3) | data formatting | bytes 393216 | tf_op jit(solution)/shard_map/reshape.14
  65.2 4.5 %all_gather.13 = bf16[1,64,768]{2,1,0:T(8,128)(2,1)S(1)} all-gather(bf16[1,32,768]{2,1,0:T(8,128)(2,1)S(1)} %convert_element_type.76), channel_id=1, replica_groups=mesh['groups'=2,'chol'=4,'walk'=2,'kpt'=2] {'kpt'}, dimensions={1}, use_global_device_ids=true | all-gather | bytes 147456 | tf_op jit(solution)/shard_map/all_gather | solution.py:59
  69.7 0.9 %gather_fusion.1 = bf16[128,768]{1,0:T(8,128)(2,1)S(1)} fusion(bf16[64,768]{1,0:T(8,128)(2,1)S(1)} %bitcast.90, s32[1024]{0:T(1024)S(1)} %pad_clamp_fusion), kind=kCustom, calls=%fused_computation.1.clone | custom fusion | bytes 393728 | tf_op jit(solution)/shard_map/jit(_take)/gather | solution.py:60
  70.7 1.7 %reshape.162 = bf16[32,4,32,24]{3,2,0,1:T(8,128)(2,1)S(1)} reshape(bf16[1,32,4,768]{3,1,2,0:T(8,128)(2,1)S(1)} %copy_select_fusion.2) | data formatting | bytes 393216 | tf_op jit(solution)/shard_map/reshape.39
  73.4 2.1 %all_gather.14 = bf16[1,64,768]{2,1,0:T(8,128)(2,1)S(1)} all-gather(bf16[1,32,768]{2,1,0:T(8,128)(2,1)S(1)} %convert_element_type.77), channel_id=1, replica_groups=mesh['groups'=2,'chol'=4,'walk'=2,'kpt'=2] {'kpt'}, dimensions={1}, use_global_device_ids=true | all-gather | bytes 147456 | tf_op jit(solution)/shard_map/all_gather | solution.py:59
  75.5 0.9 %gather_fusion.2 = bf16[128,768]{1,0:T(8,128)(2,1)S(1)} fusion(bf16[64,768]{1,0:T(8,128)(2,1)S(1)} %bitcast.91, s32[1024]{0:T(1024)S(1)} %pad_clamp_fusion), kind=kCustom, calls=%fused_computation.2.clone | custom fusion | bytes 393728 | tf_op jit(solution)/shard_map/jit(_take)/gather | solution.py:60
  76.5 1.7 %reshape.164 = bf16[32,4,32,24]{3,2,0,1:T(8,128)(2,1)S(1)} reshape(bf16[1,32,4,768]{3,1,2,0:T(8,128)(2,1)S(1)} %copy_select_fusion.1) | data formatting | bytes 393216 | tf_op jit(solution)/shard_map/reshape.42
  79.2 1.9 %all_gather.15 = bf16[1,64,768]{2,1,0:T(8,128)(2,1)S(1)} all-gather(bf16[1,32,768]{2,1,0:T(8,128)(2,1)S(1)} %convert_element_type.78), channel_id=1, replica_groups=mesh['groups'=2,'chol'=4,'walk'=2,'kpt'=2] {'kpt'}, dimensions={1}, use_global_device_ids=true | all-gather | bytes 147456 | tf_op jit(solution)/shard_map/all_gather | solution.py:59
  81.1 0.9 %gather_fusion.3 = bf16[128,768]{1,0:T(8,128)(2,1)S(1)} fusion(bf16[64,768]{1,0:T(8,128)(2,1)S(1)} %bitcast.89, s32[1024]{0:T(1024)S(1)} %pad_clamp_fusion), kind=kCustom, calls=%fused_computation.3.clone | custom fusion | bytes 393728 | tf_op jit(solution)/shard_map/jit(_take)/gather | solution.py:60
  82.1 1.7 %reshape.166 = bf16[32,4,32,24]{3,2,0,1:T(8,128)(2,1)S(1)} reshape(bf16[1,32,4,768]{3,1,2,0:T(8,128)(2,1)S(1)} %copy_select_fusion) | data formatting | bytes 393216 | tf_op jit(solution)/shard_map/reshape.45
  (43 shorter events, 9.6 us)
Async XLA Ops:
  15.4 7.5 %all-to-all-start.1 = ((bf16[2,2,32768]{2,1,0:T(2,128)(2,1)}), bf16[2,2,32768]{2,1,0:T(2,128)(2,1)S(1)}, u32[]{:S(2)}, u32[]{:S(2)}) async-start(bf16[2,2,32768]{2,1,0:T(2,128)(2,1)} %reshape.244), calls=%async_computation.1 | async-start | bytes 524288 | tf_op jit(solution)/shard_map/all_to_all | solution.py:29
  24.2 32.6 %copy-start.1 = (s32[64,4]{0,1:T(4,128)S(1)}, s32[64,4]{0,1:T(4,128)}, u32[]{:S(2)}) copy-start(s32[64,4]{0,1:T(4,128)} %param.11) | copy-start | bytes 3076
  24.2 32.9 %copy-start = (bf16[1,32,768]{2,1,0:T(8,128)(2,1)S(1)}, bf16[1,32,768]{2,1,0:T(8,128)(2,1)}, u32[]{:S(2)}) copy-start(bf16[1,32,768]{2,1,0:T(8,128)(2,1)} %param.10) | copy-start | bytes 147460
  44.3 7.9 %all-to-all-start.2 = ((bf16[8,1,32,512]{3,2,1,0:T(8,128)(2,1)}), bf16[8,1,32,512]{3,2,1,0:T(8,128)(2,1)S(1)}, u32[]{:S(2)}, u32[]{:S(2)}) async-start(bf16[8,1,32,512]{3,2,1,0:T(8,128)(2,1)} %copy.41), calls=%async_computation.2 | async-start | bytes 524288 | tf_op jit(solution)/shard_map/all_to_all | solution.py:51
  53.4 10.2 %all-to-all-start.3 = ((bf16[4,1,32,1024]{3,2,1,0:T(8,128)(2,1)}), bf16[4,1,32,1024]{3,2,1,0:T(8,128)(2,1)S(1)}, u32[]{:S(2)}, u32[]{:S(2)}) async-start(bf16[4,1,32,1024]{3,2,1,0:T(8,128)(2,1)} %all_to_all.48), calls=%async_computation.3 | async-start | bytes 524288 | tf_op jit(solution)/shard_map/all_to_all | solution.py:52
where the time goes:
time: 86.3 us; the launch traced here: 85.4 us
  blocking collectives  33 us (38%)
  local copies, waits for them, and re-layouts  20.2 us (23%)
  matrix products  12.2 us (14%)
  starting transfers between devices  10.3 us (12%)
  waiting for transfers between devices  7.77 us (9%)
  other arithmetic  1.13 us (1%)
  between operations  0.87 us (1%)
    all_to_all x1, blocking collectives, per_device(): lax.all_to_all(green_blocks, 'chol', split_axis=1, concat_axis=0, tiled=T...  12.3 us
    all_gather x4, blocking collectives, per_device(): gathered = lax.all_gather(series_term, 'kpt', axis=1, tiled=True)  11.6 us
    psum x1, blocking collectives, per_device(): lax.psum(partial_bias.astype(jnp.bfloat16), ('walk', 'kpt'))  9.09 us
    another operation x5, local copies, waits for them, and re-layouts  7.3 us
    dot_general x1, matrix products, per_device(): jnp.einsum('wqn,qxn->wqx', shifted, vector_rows, preferred_element_type=j...  5.64 us
    dot_general x1, matrix products, per_device(): jnp.einsum('wqx,qxn->wqn', arrived.reshape(everyone, local_transfers, kpt...  4.59 us
    all_to_all x1, waiting for transfers between devices, per_device(): lax.all_to_all(outgoing, 'walk', split_axis=0, concat_axis=3, tiled=True)  4.47 us
    gather x8, local copies, waits for them, and re-layouts, per_device(): jnp.take(gathered, local_table, axis=1)  3.69 us
  transfers between devices with their start and end apart: 3, of which 2 were waited for; matrix products, arithmetic and copies ran while one was open for 5% of the time, Pallas kernels for 0%

commit v1 on v0

v1 whole, which is shorter than its diff:
```python
import functools

import jax
import jax.numpy as jnp
from jax import lax
from jax.experimental import pallas as pl
from jax.experimental.pallas import tpu as pltpu
from jax.sharding import PartitionSpec as P

NORB = 32
SPOCC = 24
TAYLOR = 4
LANES = 128
HALF = 16
MESH = pl.DeviceIdType.MESH


bias_scale = 0.5


def repeat(count, body):
    if count <= 16:
        for step in range(count):
            body(step)
    else:
        lax.fori_loop(0, count, lambda step, carry: (body(step), carry)[1], 0)


def kernel(
    sizes,
    table_ref,
    green_ref,
    chol_ref,
    aux_ref,
    orb_ref,
    bias_out,
    orb_out,
    chol_v,
    arrived,
    parts,
    aux_v,
    bias_v,
    op_send,
    ops,
    relay,
    blocks,
    orb_v,
    total,
    term0,
    term1,
    term2,
    term3,
    chol_sem,
    small_sem,
    own_sem,
    green_send,
    green_recv,
    part_send,
    part_recv,
    op_sendsem,
    op_recv,
    term_send,
    term_recv,
):
    C, H, KD, PD, N = sizes
    W = C * H
    halves = KD // HALF
    my_c, my_h, my_k = lax.axis_index("chol"), lax.axis_index("walk"), lax.axis_index("kpt")
    me = my_c * H + my_h
    terms = (term0, term1, term2, term3)
    quads = C // 4
    chol_chunks = chol_sem.shape[0]
    chunk_k = KD // chol_chunks

    orb_copy = pltpu.make_async_copy(orb_ref.at[0], orb_v, small_sem.at[0])
    orb_copy.start()
    aux_copy = pltpu.make_async_copy(aux_ref, aux_v, small_sem.at[1])
    aux_copy.start()

    def chol_copy(chunk):
        rows = pl.ds(chunk * chunk_k, chunk_k)
        return pltpu.make_async_copy(chol_ref.at[0, rows], chol_v.at[rows], chol_sem.at[chunk])

    def own_green(half):
        rows = pl.ds(half * HALF, HALF)
        slab = pl.ds(pl.multiple_of(my_h * PD, PD), PD)
        return pltpu.make_async_copy(
            green_ref.at[0, my_c, rows, slab], arrived.at[me, rows], own_sem.at[half]
        )

    barrier = pltpu.get_barrier_semaphore()

    def greet(step):
        peer = lax.rem(me + 1 + step, W)
        pl.semaphore_signal(
            barrier, inc=1, device_id={"chol": peer // H, "walk": lax.rem(peer, H)}, device_id_type=MESH
        )

    repeat(W - 1, greet)

    def greet_other(step):
        pl.semaphore_signal(
            barrier, inc=1, device_id={"walk": step, "kpt": 1 - my_k}, device_id_type=MESH
        )

    repeat(H, greet_other)
    for half in range(halves):
        own_green(half).start()
    pl.semaphore_wait(barrier, W - 1 + H)

    def green_copy(half, step):
        peer = lax.rem(me + 1 + step, W)
        pc, ph = peer // H, lax.rem(peer, H)
        rows = pl.ds(half * HALF, HALF)
        slab = pl.ds(pl.multiple_of(ph * PD, PD), PD)
        return pltpu.make_async_remote_copy(
            src_ref=green_ref.at[0, pc, rows, slab],
            dst_ref=arrived.at[me, rows],
            send_sem=green_send.at[half, step],
            recv_sem=green_recv.at[half, me],
            device_id={"chol": pc, "walk": ph},
            device_id_type=MESH,
        )

    def green_wait(half, step):
        peer = lax.rem(me + 1 + step, W)
        pc, ph = peer // H, lax.rem(peer, H)
        rows = pl.ds(half * HALF, HALF)
        pltpu.make_async_remote_copy(
            src_ref=arrived.at[peer, rows],
            dst_ref=arrived.at[peer, rows],
            send_sem=green_send.at[half, step],
            recv_sem=green_recv.at[half, peer],
            device_id={"chol": pc, "walk": ph},
            device_id_type=MESH,
        ).wait_recv()

    for half in range(halves):
        repeat(W - 1, lambda step: green_copy(half, step).start())
    for chunk in range(chol_chunks):
        chol_copy(chunk).start()

    lane = lax.broadcasted_iota(jnp.int32, (KD, LANES), 1)
    orb_copy.wait()
    for l in range(NORB):
        v, off = divmod(l * SPOCC, LANES)
        shift = (LANES - off) % LANES
        piece = orb_v[:, v * LANES : (v + 1) * LANES].astype(jnp.float32)
        if shift:
            piece = pltpu.roll(piece, shift, 1)
        if off + SPOCC > LANES:
            following = orb_v[:, (v + 1) * LANES : (v + 2) * LANES].astype(jnp.float32)
            piece = jnp.where(lane < LANES - off, piece, pltpu.roll(following, shift, 1))
        relay[l * KD : (l + 1) * KD, :] = jnp.where(lane < SPOCC, piece, 0.0)
    for k in range(KD):
        rows = relay[pl.ds(k, NORB, stride=KD), :]
        total[k] = rows
        term0[my_k * KD + k] = rows.astype(jnp.bfloat16)

    chunks = 4
    per_chunk = KD // chunks

    def term_copy(degree, chunk):
        rows = pl.ds(my_k * KD + chunk * per_chunk, per_chunk)
        return pltpu.make_async_remote_copy(
            src_ref=terms[degree].at[rows],
            dst_ref=terms[degree].at[rows],
            send_sem=term_send.at[degree, chunk],
            recv_sem=term_recv.at[degree, chunk],
            device_id={"kpt": 1 - my_k},
            device_id_type=MESH,
        )

    def term_wait(degree, chunk):
        rows = pl.ds((1 - my_k) * KD + chunk * per_chunk, per_chunk)
        pltpu.make_async_remote_copy(
            src_ref=terms[degree].at[rows],
            dst_ref=terms[degree].at[rows],
            send_sem=term_send.at[degree, chunk],
            recv_sem=term_recv.at[degree, chunk],
            device_id={"kpt": 1 - my_k},
            device_id_type=MESH,
        ).wait_recv()

    for chunk in range(chunks):
        term_copy(0, chunk).start()

    partial = jnp.zeros((W, N), jnp.float32)
    for half in range(halves):
        own_green(half).wait()
        repeat(W - 1, lambda step: green_wait(half, step))
        k0 = half * HALF
        for chunk in range(chol_chunks // halves):
            chol_copy(half * (chol_chunks // halves) + chunk).wait()
        for group in range(0, HALF, 8):
            rows = arrived[:, k0 : k0 + HALF, :].astype(jnp.float32)[:, group : group + 8, :]
            rows = jnp.swapaxes(rows, 0, 1)
            left = jnp.concatenate([rows[k] for k in range(8)], axis=1).astype(jnp.bfloat16)
            right = chol_v[k0 + group : k0 + group + 8].reshape(8 * PD, N)
            partial += jnp.dot(left, right, preferred_element_type=jnp.float32)

    slot = my_h * 2 + my_k
    parts[slot] = partial

    def part_copy(step):
        peer = lax.rem(slot + 1 + step, 2 * H)
        return pltpu.make_async_remote_copy(
            src_ref=parts.at[slot],
            dst_ref=parts.at[slot],
            send_sem=part_send.at[step],
            recv_sem=part_recv.at[slot],
            device_id={"walk": peer // 2, "kpt": lax.rem(peer, 2)},
            device_id_type=MESH,
        )

    def part_wait(step):
        peer = lax.rem(slot + 1 + step, 2 * H)
        pltpu.make_async_remote_copy(
            src_ref=parts.at[peer],
            dst_ref=parts.at[peer],
            send_sem=part_send.at[step],
            recv_sem=part_recv.at[peer],
            device_id={"walk": peer // 2, "kpt": lax.rem(peer, 2)},
            device_id_type=MESH,
        ).wait_recv()

    repeat(2 * H - 1, lambda step: part_copy(step).start())
    aux_copy.wait()
    fields = aux_v[:, 0, :]
    repeat(2 * H - 1, part_wait)
    bias = parts[0]
    for other in range(1, 2 * H):
        bias += parts[other]
    shifted = (fields - jnp.clip(-bias_scale * bias, -1.0, 1.0)).astype(jnp.bfloat16)

    def op_copy(half, step):
        peer = lax.rem(me + 1 + step, W)
        pc, ph = peer // H, lax.rem(peer, H)
        rows = pl.ds(half * HALF, HALF)
        slab = pl.ds(pl.multiple_of(my_h * PD, PD), PD)
        return pltpu.make_async_remote_copy(
            src_ref=op_send.at[peer, rows],
            dst_ref=ops.at[my_c, rows, slab],
            send_sem=op_sendsem.at[half, step],
            recv_sem=op_recv.at[half, me],
            device_id={"chol": pc, "walk": ph},
            device_id_type=MESH,
        )

    def op_wait(half, step):
        peer = lax.rem(me + 1 + step, W)
        pc, ph = peer // H, lax.rem(peer, H)
        rows = pl.ds(half * HALF, HALF)
        slab = pl.ds(pl.multiple_of(ph * PD, PD), PD)
        pltpu.make_async_remote_copy(
            src_ref=op_send.at[peer, rows],
            dst_ref=ops.at[pc, rows, slab],
            send_sem=op_sendsem.at[half, step],
            recv_sem=op_recv.at[half, peer],
            device_id={"chol": pc, "walk": ph},
            device_id_type=MESH,
        ).wait_recv()

    def own_op(half):
        rows = pl.ds(half * HALF, HALF)
        slab = pl.ds(pl.multiple_of(my_h * PD, PD), PD)
        return pltpu.make_async_copy(
            op_send.at[me, rows], ops.at[my_c, rows, slab], own_sem.at[half]
        )

    for half in range(halves):
        k0 = half * HALF
        pieces = []
        for group in range(0, HALF, 8):
            right = chol_v[k0 + group : k0 + group + 8].reshape(8 * PD, N)
            out = lax.dot_general(
                shifted, right, (((1,), (1,)), ((), ())), preferred_element_type=jnp.float32
            )
            stacked = jnp.stack([out[:, k * PD : (k + 1) * PD] for k in range(8)], axis=0)
            pieces.append(jnp.swapaxes(stacked, 0, 1))
        op_send[:, k0 : k0 + HALF, :] = jnp.concatenate(pieces, axis=1).astype(jnp.bfloat16)
        repeat(W - 1, lambda step: op_copy(half, step).start())
        own_op(half).start()

    bias_v[:, 0, :] = bias
    bias_copy = pltpu.make_async_copy(bias_v, bias_out, small_sem.at[1])
    bias_copy.start()

    narrow = lax.broadcasted_iota(jnp.int32, (HALF, LANES), 1) // NORB
    for half in range(halves):
        k0 = half * HALF
        own_op(half).wait()
        repeat(W - 1, lambda step: op_wait(half, step))
        for quad in range(quads):
            for tile in range(NORB * NORB // LANES):
                given = [
                    ops[4 * quad + j, k0 : k0 + HALF, tile * LANES : (tile + 1) * LANES].astype(jnp.float32)
                    for j in range(4)
                ]
                for inner in range(4):
                    made = None
                    for j in range(4):
                        turn = (j - inner) % 4 * NORB
                        value = pltpu.roll(given[j], turn, 1) if turn else given[j]
                        made = value if made is None else jnp.where(narrow == j, value, made)
                    row = (tile * 4 + inner) * HALF
                    relay[row : row + HALF, :] = made
            for k in range(HALF):
                rows = relay[pl.ds(k, NORB, stride=HALF), :]
                blocks[k0 + k, :, quad * LANES : (quad + 1) * LANES] = rows.astype(jnp.bfloat16)

    for degree in range(1, TAYLOR + 1):
        source = terms[degree - 1]
        for chunk in range(chunks):
            term_wait(degree - 1, chunk)
        for chunk in range(chunks):
            for inner in range(per_chunk):
                k = chunk * per_chunk + inner
                right = jnp.concatenate(
                    [source[table_ref[my_k * KD + k, j]] for j in range(C)], axis=0
                )
                update = jnp.dot(blocks[k], right, preferred_element_type=jnp.float32)
                if degree > 1:
                    update = update * (1.0 / degree)
                total[k] += update
                if degree < TAYLOR:
                    terms[degree][my_k * KD + k] = update.astype(jnp.bfloat16)
            if degree < TAYLOR:
                term_copy(degree, chunk).start()

    made = [jnp.zeros((KD, LANES), jnp.float32) for _ in range(NORB * SPOCC // LANES)]
    flat = total.reshape(KD * NORB, LANES)
    for i in range(NORB):
        v, off = divmod(i * SPOCC, LANES)
        rows = flat[pl.ds(i, KD, stride=NORB), :]
        if off:
            rows = pltpu.roll(rows, off, 1)
        if off + SPOCC > LANES:
            made[v] += jnp.where(lane >= off, rows, 0.0)
            made[v + 1] += jnp.where(lane < off, rows, 0.0)
        else:
            made[v] += rows
    orb_v[...] = jnp.concatenate(made, axis=1).astype(jnp.bfloat16)
    result = pltpu.make_async_copy(orb_v, orb_out.at[0], small_sem.at[0])
    result.start()

    for half in range(halves):
        repeat(W - 1, lambda step: green_copy(half, step).wait_send())
        repeat(W - 1, lambda step: op_copy(half, step).wait_send())
    repeat(2 * H - 1, lambda step: part_copy(step).wait_send())
    for degree in range(TAYLOR):
        for chunk in range(chunks):
            term_copy(degree, chunk).wait_send()
    bias_copy.wait()
    result.wait()


def per_device(green_blocks, chol_vectors, aux_fields, orbitals, transfer_table):
    C = lax.axis_size("chol")
    H = lax.axis_size("walk")
    KD = green_blocks.shape[2]
    PD = chol_vectors.shape[2]
    N = chol_vectors.shape[3]
    K = transfer_table.shape[0]
    W = C * H
    anywhere = pl.BlockSpec(memory_space=pl.ANY)
    halves = KD // HALF
    chol_chunks = 4
    term = pltpu.VMEM((K, NORB, LANES), jnp.bfloat16)
    dma = pltpu.SemaphoreType.DMA
    return pl.pallas_call(
        functools.partial(kernel, (C, H, KD, PD, N)),
        out_shape=(
            jax.ShapeDtypeStruct(aux_fields.shape, jnp.float32),
            jax.ShapeDtypeStruct(orbitals.shape, jnp.bfloat16),
        ),
        in_specs=[pl.BlockSpec(memory_space=pltpu.SMEM)] + [anywhere] * 4,
        out_specs=(anywhere, anywhere),
        scratch_shapes=[
            pltpu.VMEM((KD, PD, N), jnp.bfloat16),
            pltpu.VMEM((W, KD, PD), jnp.bfloat16),
            pltpu.VMEM((2 * H, W, N), jnp.float32),
            pltpu.VMEM((W, 1, N), jnp.float32),
            pltpu.VMEM((W, 1, N), jnp.float32),
            pltpu.VMEM((W, KD, PD), jnp.bfloat16),
            pltpu.VMEM((C, KD, NORB * NORB), jnp.bfloat16),
            pltpu.VMEM((NORB * KD, LANES), jnp.float32),
            pltpu.VMEM((KD, NORB, C * NORB), jnp.bfloat16),
            pltpu.VMEM((KD, NORB * SPOCC), jnp.bfloat16),
            pltpu.VMEM((KD, NORB, LANES), jnp.float32),
            term,
            term,
            term,
            term,
            dma((chol_chunks,)),
            dma((2,)),
            dma((halves,)),
            dma((halves, W)),
            dma((halves, W)),
            dma((2 * H,)),
            dma((2 * H,)),
            dma((halves, W)),
            dma((halves, W)),
            dma((TAYLOR, 4)),
            dma((TAYLOR, 4)),
        ],
        compiler_params=pltpu.CompilerParams(
            collective_id=0, has_side_effects=True, vmem_limit_bytes=48 * 1024 * 1024
        ),
        name="walker_step",
    )(transfer_table, green_blocks, chol_vectors, aux_fields, orbitals)


def solution(mesh):
    placed = (
        P(("groups", "chol", "walk"), None, "kpt", None),
        P("chol", "kpt", "walk", None),
        P("groups", "chol", None),
        P(("groups", "chol", "walk"), "kpt", None),
        P(),
    )
    return jax.shard_map(
        per_device,
        mesh=mesh,
        in_specs=placed,
        out_specs=(P("groups", "chol", None), P(("groups", "chol", "walk"), "kpt", None)),
        check_vma=False,
    )
```

time: 86.3 us -> 39.1 us (0.45)
  Pallas kernels: 0 us -> 33.7 us
  blocking collectives: 33 us -> 0 us
  local copies, waits for them, and re-layouts: 20.2 us -> 4.44 us
  matrix products: 12.2 us -> 0 us
  starting transfers between devices: 10.3 us -> 0 us
  waiting for transfers between devices: 7.77 us -> 0 us
  other arithmetic: 1.13 us -> 0 us
    pallas_call x0 -> x1, Pallas kernels: none -> 33.7 us  [per_device(): pl.pallas_call(functools.partial(kernel, (C, H, KD, PD, N)), out_shape=(j...]
    all_to_all x1 -> x0, blocking collectives: 12.3 us -> none  [per_device(): lax.all_to_all(green_blocks, 'chol', split_axis=1, concat_axis=0, tiled=T...]
    dot_general x6 -> x0, matrix products: 12.2 us -> none  [the longest x1 5.64 us: per_device(): jnp.einsum('wqn,qxn->wqx', shifted, vector_rows, preferred_element_type=j...]
    all_gather x4 -> x0, blocking collectives: 11.6 us -> none  [per_device(): gathered = lax.all_gather(series_term, 'kpt', axis=1, tiled=True)]
    all_to_all x3 -> x0, starting transfers between devices: 10.3 us -> none  [the longest x1 3.44 us: per_device(): lax.all_to_all(lax.all_to_all(green_blocks, 'chol', split_axis=1, concat_...]
    psum x1 -> x0, blocking collectives: 9.09 us -> none  [per_device(): lax.psum(partial_bias.astype(jnp.bfloat16), ('walk', 'kpt'))]
    all_to_all x3 -> x0, waiting for transfers between devices: 7.77 us -> none  [the longest x1 4.47 us: per_device(): lax.all_to_all(outgoing, 'walk', split_axis=0, concat_axis=3, tiled=True)]
    another operation x5 -> x0, local copies, waits for them, and re-layouts: 7.3 us -> none
  transfers between devices with their start and end apart: 3 -> 0, of which waited for: 2 -> 0; matrix products, arithmetic and copies ran while one was open for 5% -> 0% of each run, Pallas kernels for 0% -> 0%
where the time goes in v1:
time: 39.1 us; the launch traced here: 38.8 us
  Pallas kernels  33.7 us (86%)
  local copies, waits for them, and re-layouts  4.44 us (11%)
  between operations  0.64 us (2%)
    pallas_call x1, Pallas kernels, per_device(): pl.pallas_call(functools.partial(kernel, (C, H, KD, PD, N)), out_shape=(j...  33.7 us
    unnamed x9, local copies, waits for them, and re-layouts  4.44 us

profile of v1, /device:TPU:1, one launch (start us, length us, event | category | flops | bytes accessed | tf_op | source)
XLA Modules:
  0.0 38.8 jit_solution(502224414322344903)
XLA Ops:
  0.6 0.8 %copy.7.table_ref = s32[64,4]{1,0:T(8,128)S(1)} copy(s32[64,4]{0,1:T(4,128)} %param.9) | data formatting | bytes 2048 | tf_op args[4]
  1.4 0.0 copy-start
  1.4 0.9 %copy-done = bf16[1,4,32,1024]{3,2,1,0:T(8,128)(2,1)S(1)} copy-done((bf16[1,4,32,1024]{3,2,1,0:T(8,128)(2,1)S(1)}, bf16[1,4,32,1024]{3,2,1,0:T(8,128)(2,1)}, u32[]{:S(2)}) %copy-start) | copy-done | bytes 262168
  2.4 0.0 copy-start.1
  2.4 0.8 %copy-done.1 = bf16[1,32,768]{2,1,0:T(8,128)(2,1)S(1)} copy-done((bf16[1,32,768]{2,1,0:T(8,128)(2,1)S(1)}, bf16[1,32,768]{2,1,0:T(8,128)(2,1)}, u32[]{:S(2)}) %copy-start.1) | copy-done | bytes 49176
  3.2 0.0 copy-start.2
  3.2 0.7 %copy-done.2 = f32[8,1,256]{2,1,0:T(1,128)S(1)} copy-done((f32[8,1,256]{2,1,0:T(1,128)S(1)}, f32[8,1,256]{2,1,0:T(1,128)}, u32[]{:S(2)}) %copy-start.2) | copy-done | bytes 8216
  3.8 33.7 %walker_step.1 = (f32[8,1,256]{2,1,0:T(1,128)S(1)}, bf16[1,32,768]{2,1,0:T(8,128)(2,1)S(1)}) custom-call(s32[64,4]{1,0:T(8,128)S(1)} %copy.7.table_ref, bf16[1,4,32,1024]{3,2,1,0:T(8,128)(2,1)S(1)} %copy-done, bf16[1,32,512,256]{3,2,1,0:T(8,128)(2,1)} %chol_ref.1, f32[8,1,256]{2,1,0:T(1,128)S(1)} %copy-done.2, bf16[1,32,768]{2,1,0:T(8,128)(2,1)S(1)} %copy-done.1), custom_call_target="tpu_custom_call" | custom-call | tf_op jit(solution)/shard_map/walker_step/pallas_call | solution.py:371
  37.6 0.6 %copy.10 = f32[8,1,256]{2,1,0:T(1,128)} copy(f32[8,1,256]{2,1,0:T(1,128)S(1)} %get-tuple-element.4) | data formatting | bytes 16384
  38.2 0.6 %copy.11 = bf16[1,32,768]{2,1,0:T(8,128)(2,1)} copy(bf16[1,32,768]{2,1,0:T(8,128)(2,1)S(1)} %get-tuple-element.5) | data formatting | bytes 98304
Async XLA Ops:
  1.4 0.9 %copy-start = (bf16[1,4,32,1024]{3,2,1,0:T(8,128)(2,1)S(1)}, bf16[1,4,32,1024]{3,2,1,0:T(8,128)(2,1)}, u32[]{:S(2)}) copy-start(bf16[1,4,32,1024]{3,2,1,0:T(8,128)(2,1)} %green_ref.1) | copy-start | bytes 786436
  2.4 0.8 %copy-start.1 = (bf16[1,32,768]{2,1,0:T(8,128)(2,1)S(1)}, bf16[1,32,768]{2,1,0:T(8,128)(2,1)}, u32[]{:S(2)}) copy-start(bf16[1,32,768]{2,1,0:T(8,128)(2,1)} %orb_ref.1) | copy-start | bytes 147460
  3.2 0.7 %copy-start.2 = (f32[8,1,256]{2,1,0:T(1,128)S(1)}, f32[8,1,256]{2,1,0:T(1,128)}, u32[]{:S(2)}) copy-start(f32[8,1,256]{2,1,0:T(1,128)} %aux_ref.1) | copy-start | bytes 24580

commit v2 on v1

--- a/solution.py
+++ b/solution.py
@@ -28,7 +28,7 @@
 
 def kernel(
     sizes,
-    table_ref,
+    table_in,
     green_ref,
     chol_ref,
     aux_ref,
@@ -39,7 +39,6 @@
     arrived,
     parts,
     aux_v,
-    bias_v,
     op_send,
     ops,
     relay,
@@ -50,6 +49,7 @@
     term1,
     term2,
     term3,
+    table_ref,
     chol_sem,
     small_sem,
     own_sem,
@@ -65,6 +65,9 @@
     C, H, KD, PD, N = sizes
     W = C * H
     halves = KD // HALF
+    splits = green_send.shape[0] // halves
+    pieces = halves * splits
+    width = PD // splits
     my_c, my_h, my_k = lax.axis_index("chol"), lax.axis_index("walk"), lax.axis_index("kpt")
     me = my_c * H + my_h
     terms = (term0, term1, term2, term3)
@@ -72,71 +75,88 @@
     chol_chunks = chol_sem.shape[0]
     chunk_k = KD // chol_chunks
 
+    top, low = my_c // (C // 2), lax.rem(my_c, C // 2)
+
+    def peer_at(step):
+        near = step // (W // 2)
+        rest = step % (W // 2) + near
+        pc = lax.rem(top + 1 - near, 2) * (C // 2) + lax.rem(low + rest // H, C // 2)
+        ph = lax.rem(my_h + rest % H, H)
+        return pc, ph, pc * H + ph
+
+    def rows_of(piece):
+        return pl.ds(piece // splits * HALF, HALF)
+
+    def slab_of(h, piece):
+        start = h * PD + piece % splits * width
+        return pl.ds(pl.multiple_of(start, LANES), width)
+
+    def part_of(piece):
+        return pl.ds(piece % splits * width, width)
+
+    barrier = pltpu.get_barrier_semaphore()
+
+    def greet(step):
+        pc, ph, _ = peer_at(step)
+        pl.semaphore_signal(barrier, inc=1, device_id={"chol": pc, "walk": ph}, device_id_type=MESH)
+
+    repeat(W - 1, greet)
+
+    def greet_other(step):
+        pl.semaphore_signal(
+            barrier, inc=1, device_id={"walk": step, "kpt": 1 - my_k}, device_id_type=MESH
+        )
+
+    repeat(H, greet_other)
     orb_copy = pltpu.make_async_copy(orb_ref.at[0], orb_v, small_sem.at[0])
     orb_copy.start()
     aux_copy = pltpu.make_async_copy(aux_ref, aux_v, small_sem.at[1])
     aux_copy.start()
+    table_copy = pltpu.make_async_copy(table_in, table_ref, small_sem.at[2])
+    table_copy.start()
 
     def chol_copy(chunk):
         rows = pl.ds(chunk * chunk_k, chunk_k)
         return pltpu.make_async_copy(chol_ref.at[0, rows], chol_v.at[rows], chol_sem.at[chunk])
 
-    def own_green(half):
-        rows = pl.ds(half * HALF, HALF)
-        slab = pl.ds(pl.multiple_of(my_h * PD, PD), PD)
+    def own_green(piece):
+        rows = rows_of(piece)
         return pltpu.make_async_copy(
-            green_ref.at[0, my_c, rows, slab], arrived.at[me, rows], own_sem.at[half]
-        )
-
-    barrier = pltpu.get_barrier_semaphore()
-
-    def greet(step):
-        peer = lax.rem(me + 1 + step, W)
-        pl.semaphore_signal(
-            barrier, inc=1, device_id={"chol": peer // H, "walk": lax.rem(peer, H)}, device_id_type=MESH
-        )
-
-    repeat(W - 1, greet)
-
-    def greet_other(step):
-        pl.semaphore_signal(
-            barrier, inc=1, device_id={"walk": step, "kpt": 1 - my_k}, device_id_type=MESH
-        )
-
-    repeat(H, greet_other)
-    for half in range(halves):
-        own_green(half).start()
+            green_ref.at[0, my_c, rows, slab_of(my_h, piece)],
+            arrived.at[me, rows, part_of(piece)],
+            own_sem.at[piece],
+        )
+
+    for piece in range(pieces):
+        own_green(piece).start()
     pl.semaphore_wait(barrier, W - 1 + H)
 
-    def green_copy(half, step):
-        peer = lax.rem(me + 1 + step, W)
-        pc, ph = peer // H, lax.rem(peer, H)
-        rows = pl.ds(half * HALF, HALF)
-        slab = pl.ds(pl.multiple_of(ph * PD, PD), PD)
+    def green_copy(piece, step):
+        pc, ph, _ = peer_at(step)
+        rows = rows_of(piece)
         return pltpu.make_async_remote_copy(
-            src_ref=green_ref.at[0, pc, rows, slab],
-            dst_ref=arrived.at[me, rows],
-            send_sem=green_send.at[half, step],
-            recv_sem=green_recv.at[half, me],
+            src_ref=green_ref.at[0, pc, rows, slab_of(ph, piece)],
+            dst_ref=arrived.at[me, rows, part_of(piece)],
+            send_sem=green_send.at[piece, step],
+            recv_sem=green_recv.at[piece, me],
             device_id={"chol": pc, "walk": ph},
             device_id_type=MESH,
         )
 
-    def green_wait(half, step):
-        peer = lax.rem(me + 1 + step, W)
-        pc, ph = peer // H, lax.rem(peer, H)
-        rows = pl.ds(half * HALF, HALF)
+    def green_wait(piece, step):
+        pc, ph, peer = peer_at(step)
+        landed = arrived.at[peer, rows_of(piece), part_of(piece)]
         pltpu.make_async_remote_copy(
-            src_ref=arrived.at[peer, rows],
-            dst_ref=arrived.at[peer, rows],
-            send_sem=green_send.at[half, step],
-            recv_sem=green_recv.at[half, peer],
+            src_ref=landed,
+            dst_ref=landed,
+            send_sem=green_send.at[piece, step],
+            recv_sem=green_recv.at[piece, peer],
             device_id={"chol": pc, "walk": ph},
             device_id_type=MESH,
         ).wait_recv()
 
-    for half in range(halves):
-        repeat(W - 1, lambda step: green_copy(half, step).start())
+    for piece in range(pieces):
+        repeat(W - 1, lambda step: green_copy(piece, step).start())
     for chunk in range(chol_chunks):
         chol_copy(chunk).start()
 
@@ -186,17 +206,19 @@
         term_copy(0, chunk).start()
 
     partial = jnp.zeros((W, N), jnp.float32)
-    for half in range(halves):
-        own_green(half).wait()
-        repeat(W - 1, lambda step: green_wait(half, step))
-        k0 = half * HALF
-        for chunk in range(chol_chunks // halves):
-            chol_copy(half * (chol_chunks // halves) + chunk).wait()
+    for piece in range(pieces):
+        own_green(piece).wait()
+        repeat(W - 1, lambda step: green_wait(piece, step))
+        half, split = divmod(piece, splits)
+        k0, p0 = half * HALF, split * width
+        if split == 0:
+            for chunk in range(chol_chunks // halves):
+                chol_copy(half * (chol_chunks // halves) + chunk).wait()
         for group in range(0, HALF, 8):
-            rows = arrived[:, k0 : k0 + HALF, :].astype(jnp.float32)[:, group : group + 8, :]
-            rows = jnp.swapaxes(rows, 0, 1)
+            rows = arrived[:, k0 : k0 + HALF, p0 : p0 + width].astype(jnp.float32)
+            rows = jnp.swapaxes(rows[:, group : group + 8, :], 0, 1)
             left = jnp.concatenate([rows[k] for k in range(8)], axis=1).astype(jnp.bfloat16)
-            right = chol_v[k0 + group : k0 + group + 8].reshape(8 * PD, N)
+            right = chol_v[k0 + group : k0 + group + 8, p0 : p0 + width].reshape(8 * width, N)
             partial += jnp.dot(left, right, preferred_element_type=jnp.float32)
 
     slot = my_h * 2 + my_k
@@ -226,6 +248,7 @@
 
     repeat(2 * H - 1, lambda step: part_copy(step).start())
     aux_copy.wait()
+    table_copy.wait()
     fields = aux_v[:, 0, :]
     repeat(2 * H - 1, part_wait)
     bias = parts[0]
@@ -233,64 +256,61 @@
         bias += parts[other]
     shifted = (fields - jnp.clip(-bias_scale * bias, -1.0, 1.0)).astype(jnp.bfloat16)
 
-    def op_copy(half, step):
-        peer = lax.rem(me + 1 + step, W)
-        pc, ph = peer // H, lax.rem(peer, H)
-        rows = pl.ds(half * HALF, HALF)
-        slab = pl.ds(pl.multiple_of(my_h * PD, PD), PD)
+    def op_copy(piece, step):
+        pc, ph, peer = peer_at(step)
+        rows = rows_of(piece)
         return pltpu.make_async_remote_copy(
-            src_ref=op_send.at[peer, rows],
-            dst_ref=ops.at[my_c, rows, slab],
-            send_sem=op_sendsem.at[half, step],
-            recv_sem=op_recv.at[half, me],
+            src_ref=op_send.at[peer, rows, part_of(piece)],
+            dst_ref=ops.at[my_c, rows, slab_of(my_h, piece)],
+            send_sem=op_sendsem.at[piece, step],
+            recv_sem=op_recv.at[piece, me],
             device_id={"chol": pc, "walk": ph},
             device_id_type=MESH,
         )
 
-    def op_wait(half, step):
-        peer = lax.rem(me + 1 + step, W)
-        pc, ph = peer // H, lax.rem(peer, H)
-        rows = pl.ds(half * HALF, HALF)
-        slab = pl.ds(pl.multiple_of(ph * PD, PD), PD)
+    def op_wait(piece, step):
+        pc, ph, peer = peer_at(step)
+        rows = rows_of(piece)
         pltpu.make_async_remote_copy(
-            src_ref=op_send.at[peer, rows],
-            dst_ref=ops.at[pc, rows, slab],
-            send_sem=op_sendsem.at[half, step],
-            recv_sem=op_recv.at[half, peer],
+            src_ref=op_send.at[peer, rows, part_of(piece)],
+            dst_ref=ops.at[pc, rows, slab_of(ph, piece)],
+            send_sem=op_sendsem.at[piece, step],
+            recv_sem=op_recv.at[piece, peer],
             device_id={"chol": pc, "walk": ph},
             device_id_type=MESH,
         ).wait_recv()
 
-    def own_op(half):
-        rows = pl.ds(half * HALF, HALF)
-        slab = pl.ds(pl.multiple_of(my_h * PD, PD), PD)
+    def own_op(piece):
+        rows = rows_of(piece)
         return pltpu.make_async_copy(
-            op_send.at[me, rows], ops.at[my_c, rows, slab], own_sem.at[half]
-        )
-
-    for half in range(halves):
-        k0 = half * HALF
-        pieces = []
+            op_send.at[me, rows, part_of(piece)],
+            ops.at[my_c, rows, slab_of(my_h, piece)],
+            own_sem.at[piece],
+        )
+
+    for piece in range(pieces):
+        half, split = divmod(piece, splits)
+        k0, p0 = half * HALF, split * width
+        made = []
         for group in range(0, HALF, 8):
-            right = chol_v[k0 + group : k0 + group + 8].reshape(8 * PD, N)
+            right = chol_v[k0 + group : k0 + group + 8, p0 : p0 + width].reshape(8 * width, N)
             out = lax.dot_general(
                 shifted, right, (((1,), (1,)), ((), ())), preferred_element_type=jnp.float32
             )
-            stacked = jnp.stack([out[:, k * PD : (k + 1) * PD] for k in range(8)], axis=0)
-            pieces.append(jnp.swapaxes(stacked, 0, 1))
-        op_send[:, k0 : k0 + HALF, :] = jnp.concatenate(pieces, axis=1).astype(jnp.bfloat16)
-        repeat(W - 1, lambda step: op_copy(half, step).start())
-        own_op(half).start()
-
-    bias_v[:, 0, :] = bias
-    bias_copy = pltpu.make_async_copy(bias_v, bias_out, small_sem.at[1])
-    bias_copy.start()
+            stacked = jnp.stack([out[:, k * width : (k + 1) * width] for k in range(8)], axis=0)
+            made.append(jnp.swapaxes(stacked, 0, 1))
+        op_send[:, k0 : k0 + HALF, p0 : p0 + width] = jnp.concatenate(made, axis=1).astype(jnp.bfloat16)
+        repeat(W - 1, lambda step: op_copy(piece, step).start())
+        own_op(piece).start()
+
+    bias_out[:, 0, :] = bias
 
     narrow = lax.broadcasted_iota(jnp.int32, (HALF, LANES), 1) // NORB
     for half in range(halves):
         k0 = half * HALF
-        own_op(half).wait()
-        repeat(W - 1, lambda step: op_wait(half, step))
+        for piece in range(half * splits, (half + 1) * splits):
+            own_op(piece).wait()
+            repeat(W - 1, lambda step: op_wait(piece, step))
         for quad in range(quads):
             for tile in range(NORB * NORB // LANES):
                 given = [
@@ -317,7 +337,7 @@
             for inner in range(per_chunk):
                 k = chunk * per_chunk + inner
                 right = jnp.concatenate(
-                    [source[table_ref[my_k * KD + k, j]] for j in range(C)], axis=0
+                    [source[table_ref[j, my_k * KD + k]] for j in range(C)], axis=0
                 )
                 update = jnp.dot(blocks[k], right, preferred_element_type=jnp.float32)
                 if degree > 1:
@@ -340,19 +360,14 @@
             made[v + 1] += jnp.where(lane < off, rows, 0.0)
         else:
             made[v] += rows
-    orb_v[...] = jnp.concatenate(made, axis=1).astype(jnp.bfloat16)
-    result = pltpu.make_async_copy(orb_v, orb_out.at[0], small_sem.at[0])
-    result.start()
-
-    for half in range(halves):
-        repeat(W - 1, lambda step: green_copy(half, step).wait_send())
-        repeat(W - 1, lambda step: op_copy(half, step).wait_send())
+    orb_out[0] = jnp.concatenate(made, axis=1).astype(jnp.bfloat16)
+    for piece in range(pieces):
+        repeat(W - 1, lambda step: green_copy(piece, step).wait_send())
+        repeat(W - 1, lambda step: op_copy(piece, step).wait_send())
     repeat(2 * H - 1, lambda step: part_copy(step).wait_send())
     for degree in range(TAYLOR):
         for chunk in range(chunks):
             term_copy(degree, chunk).wait_send()
-    bias_copy.wait()
-    result.wait()
 
 
 def per_device(green_blocks, chol_vectors, aux_fields, orbitals, transfer_table):
@@ -363,24 +378,24 @@
     N = chol_vectors.shape[3]
     K = transfer_table.shape[0]
     W = C * H
-    anywhere = pl.BlockSpec(memory_space=pl.ANY)
-    halves = KD // HALF
+    anywhere = pl.BlockSpec(memory_space=pltpu.HBM)
+    pieces = KD // HALF * max(1, PD // 256)
     chol_chunks = 4
     term = pltpu.VMEM((K, NORB, LANES), jnp.bfloat16)
     dma = pltpu.SemaphoreType.DMA
+    held = pl.BlockSpec(memory_space=pltpu.VMEM)
     return pl.pallas_call(
         functools.partial(kernel, (C, H, KD, PD, N)),
         out_shape=(
-            jax.ShapeDtypeStruct(aux_fields.shape, jnp.float32),
-            jax.ShapeDtypeStruct(orbitals.shape, jnp.bfloat16),
+            pltpu.VMEM(aux_fields.shape, jnp.float32),
+            pltpu.VMEM(orbitals.shape, jnp.bfloat16),
         ),
-        in_specs=[pl.BlockSpec(memory_space=pltpu.SMEM)] + [anywhere] * 4,
-        out_specs=(anywhere, anywhere),
+        in_specs=[anywhere] * 5,
+        out_specs=(held, held),
         scratch_shapes=[
             pltpu.VMEM((KD, PD, N), jnp.bfloat16),
             pltpu.VMEM((W, KD, PD), jnp.bfloat16),
             pltpu.VMEM((2 * H, W, N), jnp.float32),
-            pltpu.VMEM((W, 1, N), jnp.float32),
             pltpu.VMEM((W, 1, N), jnp.float32),
             pltpu.VMEM((W, KD, PD), jnp.bfloat16),
             pltpu.VMEM((C, KD, NORB * NORB), jnp.bfloat16),
@@ -392,24 +407,24 @@
             term,
             term,
             term,
+            pltpu.SMEM(transfer_table.shape[::-1], jnp.int32),
             dma((chol_chunks,)),
-            dma((2,)),
-            dma((halves,)),
-            dma((halves, W)),
-            dma((halves, W)),
+            dma((3,)),
+            dma((pieces,)),
+            dma((pieces, W)),
+            dma((pieces, W)),
             dma((2 * H,)),
             dma((2 * H,)),
-            dma((halves, W)),
-            dma((halves, W)),
+            dma((pieces, W)),
+            dma((pieces, W)),
             dma((TAYLOR, 4)),
             dma((TAYLOR, 4)),
         ],
         compiler_params=pltpu.CompilerParams(
-            collective_id=0, has_side_effects=True, vmem_limit_bytes=48 * 1024 * 1024
+            collective_id=0, has_side_effects=True, vmem_limit_bytes=63 * 1024 * 1024
         ),
         name="walker_step",
-    )(transfer_table, green_blocks, chol_vectors, aux_fields, orbitals)
-
+    )(transfer_table.T, green_blocks, chol_vectors, aux_fields, orbitals)
 
 def solution(mesh):
     placed = (

time: 39.1 us -> 35.7 us (0.913)
  local copies, waits for them, and re-layouts: 4.44 us -> 1.22 us
    unnamed x9 -> x2, local copies, waits for them, and re-layouts: 4.44 us -> 1.22 us
where the time goes in v2:
time: 35.7 us; the launch traced here: 35.5 us
  Pallas kernels  33.7 us (94%)
  local copies, waits for them, and re-layouts  1.22 us (3%)
  between operations  0.64 us (2%)
    pallas_call x1, Pallas kernels, per_device(): pl.pallas_call(functools.partial(kernel, (C, H, KD, PD, N)), out_shape=(p...  33.7 us
    unnamed x2, local copies, waits for them, and re-layouts  1.22 us

profile of v2, /device:TPU:1, one launch (start us, length us, event | category | flops | bytes accessed | tf_op | source)
XLA Modules:
  0.0 35.5 jit_solution(16184130018774979562)
XLA Ops:
  0.6 33.7 %walker_step.1 = (f32[8,1,256]{2,1,0:T(1,128)S(1)}, bf16[1,32,768]{2,1,0:T(8,128)(2,1)S(1)}) custom-call(s32[4,64]{1,0:T(4,128)} %bitcast.1, bf16[1,4,32,1024]{3,2,1,0:T(8,128)(2,1)} %green_ref.1, bf16[1,32,512,256]{3,2,1,0:T(8,128)(2,1)} %chol_ref.1, f32[8,1,256]{2,1,0:T(1,128)} %aux_ref.1, bf16[1,32,768]{2,1,0:T(8,128)(2,1)} %orb_ref.1), custom_call_target="tpu_custom_call" | custom-call | tf_op jit(solution)/shard_map/walker_step/pallas_call | solution.py:387
  34.3 0.6 %copy.9 = f32[8,1,256]{2,1,0:T(1,128)} copy(f32[8,1,256]{2,1,0:T(1,128)S(1)} %get-tuple-element.2) | data formatting | bytes 16384
  34.9 0.6 %copy.10 = bf16[1,32,768]{2,1,0:T(8,128)(2,1)} copy(bf16[1,32,768]{2,1,0:T(8,128)(2,1)S(1)} %get-tuple-element.3) | data formatting | bytes 98304

commit v3 on v2

--- a/solution.py
+++ b/solution.py
@@ -123,12 +123,14 @@
         rows = rows_of(piece)
         return pltpu.make_async_copy(
             green_ref.at[0, my_c, rows, slab_of(my_h, piece)],
-            arrived.at[me, rows, part_of(piece)],
+            arrived.at[piece, me],
             own_sem.at[piece],
         )
 
     for piece in range(pieces):
         own_green(piece).start()
+    for chunk in range(chol_chunks):
+        chol_copy(chunk).start()
     pl.semaphore_wait(barrier, W - 1 + H)
 
     def green_copy(piece, step):
@@ -136,7 +138,7 @@
         rows = rows_of(piece)
         return pltpu.make_async_remote_copy(
             src_ref=green_ref.at[0, pc, rows, slab_of(ph, piece)],
-            dst_ref=arrived.at[me, rows, part_of(piece)],
+            dst_ref=arrived.at[piece, me],
             send_sem=green_send.at[piece, step],
             recv_sem=green_recv.at[piece, me],
             device_id={"chol": pc, "walk": ph},
@@ -145,7 +147,7 @@
 
     def green_wait(piece, step):
         pc, ph, peer = peer_at(step)
-        landed = arrived.at[peer, rows_of(piece), part_of(piece)]
+        landed = arrived.at[piece, peer]
         pltpu.make_async_remote_copy(
             src_ref=landed,
             dst_ref=landed,
@@ -157,8 +159,6 @@
 
     for piece in range(pieces):
         repeat(W - 1, lambda step: green_copy(piece, step).start())
-    for chunk in range(chol_chunks):
-        chol_copy(chunk).start()
 
     lane = lax.broadcasted_iota(jnp.int32, (KD, LANES), 1)
     orb_copy.wait()
@@ -177,7 +177,7 @@
         total[k] = rows
         term0[my_k * KD + k] = rows.astype(jnp.bfloat16)
 
-    chunks = 4
+    chunks = 2
     per_chunk = KD // chunks
 
     def term_copy(degree, chunk):
@@ -215,7 +215,7 @@
             for chunk in range(chol_chunks // halves):
                 chol_copy(half * (chol_chunks // halves) + chunk).wait()
         for group in range(0, HALF, 8):
-            rows = arrived[:, k0 : k0 + HALF, p0 : p0 + width].astype(jnp.float32)
+            rows = arrived[piece].astype(jnp.float32)
             rows = jnp.swapaxes(rows[:, group : group + 8, :], 0, 1)
             left = jnp.concatenate([rows[k] for k in range(8)], axis=1).astype(jnp.bfloat16)
             right = chol_v[k0 + group : k0 + group + 8, p0 : p0 + width].reshape(8 * width, N)
@@ -260,8 +260,8 @@
         pc, ph, peer = peer_at(step)
         rows = rows_of(piece)
         return pltpu.make_async_remote_copy(
-            src_ref=op_send.at[peer, rows, part_of(piece)],
-            dst_ref=ops.at[my_c, rows, slab_of(my_h, piece)],
+            src_ref=op_send.at[piece, peer],
+            dst_ref=ops.at[piece, my_c, my_h],
             send_sem=op_sendsem.at[piece, step],
             recv_sem=op_recv.at[piece, me],
             device_id={"chol": pc, "walk": ph},
@@ -272,8 +272,8 @@
         pc, ph, peer = peer_at(step)
         rows = rows_of(piece)
         pltpu.make_async_remote_copy(
-            src_ref=op_send.at[peer, rows, part_of(piece)],
-            dst_ref=ops.at[pc, rows, slab_of(ph, piece)],
+            src_ref=op_send.at[piece, peer],
+            dst_ref=ops.at[piece, pc, ph],
             send_sem=op_sendsem.at[piece, step],
             recv_sem=op_recv.at[piece, peer],
             device_id={"chol": pc, "walk": ph},
@@ -283,8 +283,8 @@
     def own_op(piece):
         rows = rows_of(piece)
         return pltpu.make_async_copy(
-            op_send.at[me, rows, part_of(piece)],
-            ops.at[my_c, rows, slab_of(my_h, piece)],
+            op_send.at[piece, me],
+            ops.at[piece, my_c, my_h],
             own_sem.at[piece],
         )
 
@@ -299,7 +299,7 @@
             )
             stacked = jnp.stack([out[:, k * width : (k + 1) * width] for k in range(8)], axis=0)
             made.append(jnp.swapaxes(stacked, 0, 1))
-        op_send[:, k0 : k0 + HALF, p0 : p0 + width] = jnp.concatenate(made, axis=1).astype(jnp.bfloat16)
+        op_send[piece] = jnp.concatenate(made, axis=1).astype(jnp.bfloat16)
         repeat(W - 1, lambda step: op_copy(piece, step).start())
         own_op(piece).start()
 
@@ -313,8 +313,10 @@
             repeat(W - 1, lambda step: op_wait(piece, step))
         for quad in range(quads):
             for tile in range(NORB * NORB // LANES):
+                h, column = divmod(tile * LANES, PD)
+                piece, column = half * splits + column // width, column % width
                 given = [
-                    ops[4 * quad + j, k0 : k0 + HALF, tile * LANES : (tile + 1) * LANES].astype(jnp.float32)
+                    ops[piece, 4 * quad + j, h, :, column : column + LANES].astype(jnp.float32)
                     for j in range(4)
                 ]
                 for inner in range(4):
@@ -394,11 +396,11 @@
         out_specs=(held, held),
         scratch_shapes=[
             pltpu.VMEM((KD, PD, N), jnp.bfloat16),
-            pltpu.VMEM((W, KD, PD), jnp.bfloat16),
+            pltpu.VMEM((pieces, W, HALF, KD * PD // (pieces * HALF)), jnp.bfloat16),
             pltpu.VMEM((2 * H, W, N), jnp.float32),
             pltpu.VMEM((W, 1, N), jnp.float32),
-            pltpu.VMEM((W, KD, PD), jnp.bfloat16),
-            pltpu.VMEM((C, KD, NORB * NORB), jnp.bfloat16),
+            pltpu.VMEM((pieces, W, HALF, KD * PD // (pieces * HALF)), jnp.bfloat16),
+            pltpu.VMEM((pieces, C, H, HALF, KD * PD // (pieces * HALF)), jnp.bfloat16),
             pltpu.VMEM((NORB * KD, LANES), jnp.float32),
             pltpu.VMEM((KD, NORB, C * NORB), jnp.bfloat16),
             pltpu.VMEM((KD, NORB * SPOCC), jnp.bfloat16),
@@ -417,8 +419,8 @@
             dma((2 * H,)),
             dma((pieces, W)),
             dma((pieces, W)),
-            dma((TAYLOR, 4)),
-            dma((TAYLOR, 4)),
+            dma((TAYLOR, 2)),
+            dma((TAYLOR, 2)),
         ],
         compiler_params=pltpu.CompilerParams(
             collective_id=0, has_side_effects=True, vmem_limit_bytes=63 * 1024 * 1024

time: 35.7 us -> 35.1 us (0.983)
  Pallas kernels: 33.7 us -> 33.1 us
    pallas_call x1, Pallas kernels: 33.7 us -> 33.1 us  [per_device(): pl.pallas_call(functools.partial(kernel, (C, H, KD, PD, N)), out_shape=(p...]
where the time goes in v3:
time: 35.1 us; the launch traced here: 34.9 us
  Pallas kernels  33.1 us (94%)
  local copies, waits for them, and re-layouts  1.22 us (3%)
  between operations  0.64 us (2%)
    pallas_call x1, Pallas kernels, per_device(): pl.pallas_call(functools.partial(kernel, (C, H, KD, PD, N)), out_shape=(p...  33.1 us
    unnamed x2, local copies, waits for them, and re-layouts  1.22 us

profile of v3, /device:TPU:1, one launch (start us, length us, event | category | flops | bytes accessed | tf_op | source)
XLA Modules:
  0.0 34.9 jit_solution(3342469118525799568)
XLA Ops:
  0.6 33.1 %walker_step.1 = (f32[8,1,256]{2,1,0:T(1,128)S(1)}, bf16[1,32,768]{2,1,0:T(8,128)(2,1)S(1)}) custom-call(s32[4,64]{1,0:T(4,128)} %bitcast.1, bf16[1,4,32,1024]{3,2,1,0:T(8,128)(2,1)} %green_ref.1, bf16[1,32,512,256]{3,2,1,0:T(8,128)(2,1)} %chol_ref.1, f32[8,1,256]{2,1,0:T(1,128)} %aux_ref.1, bf16[1,32,768]{2,1,0:T(8,128)(2,1)} %orb_ref.1), custom_call_target="tpu_custom_call" | custom-call | tf_op jit(solution)/shard_map/walker_step/pallas_call | solution.py:389
  33.7 0.6 %copy.9 = f32[8,1,256]{2,1,0:T(1,128)} copy(f32[8,1,256]{2,1,0:T(1,128)S(1)} %get-tuple-element.2) | data formatting | bytes 16384
  34.3 0.6 %copy.10 = bf16[1,32,768]{2,1,0:T(8,128)(2,1)} copy(bf16[1,32,768]{2,1,0:T(8,128)(2,1)S(1)} %get-tuple-element.3) | data formatting | bytes 98304
